TPU v7x, 256 devices: a whole 4x4x8 slice. The times are simulated.
256 devices in a mesh: tok: 32 (over x, z_hi, core), hid: 8 (over y, z_lo).
Axes of the slice: x: 4, y: 4, z: 8 (z_hi: 4, z_lo: 2; z = z_hi * 2 + z_lo), core: 2. Of those that a mesh axis runs over, the one named last changes fastest.
Arguments:
- base: float32 [1024, 16384], P('tok', 'hid'), may hold values from -6 to 6
- source: float32 [1024, 16384], P('tok', 'hid'), may hold values from -6 to 6
- pairs: int32 [1024], replicated, may hold values from 0 to 1023, each once
- counts: int32 [1024], replicated, may hold values from 1 to 128
- rotation: float32 [16384, 16384], P('hid', 'tok'), may hold values from -0.046875 to 0.046875
Outputs:
- patched: float32 [1024, 16384], P('tok', 'hid')
All inputs are finite; a program needn't handle non-finite values.
Results may differ from a plain program's by a relative error of at most 0.000075.
Values sent between devices are 32-bit elements; how exact they have to be, the bound alone decides.
No kernel may reach another device: no remote copies, remote signals or barrier semaphores. Data moves between devices by JAX's collectives and lax.ppermute only.
A program may use at most 64 MiB of HBM per device.

v0:
```python
import jax
import jax.numpy as jnp
from jax import lax
from jax.sharding import PartitionSpec as P

BLOCK = 128


def local(base, source, pairs, counts, rotation):
    highest = lax.Precision.HIGHEST
    stacked = jnp.stack([base, source])
    terms = jnp.einsum(
        "srk,kc->src",
        lax.all_gather(stacked, "tok", axis=1, tiled=True),
        rotation,
        precision=highest,
        preferred_element_type=jnp.float32,
    )
    base_terms = terms[0]
    source_terms = jnp.take(terms[1], pairs, axis=0)
    width = rotation.shape[1]
    columns = lax.axis_index("tok") * width + jnp.arange(width, dtype=jnp.int32)
    summed = (
        lax.psum_scatter(base_terms, "hid", scatter_dimension=0, tiled=True),
        lax.psum_scatter(source_terms, "hid", scatter_dimension=0, tiled=True),
    )
    share = summed[0].shape[0]
    first = lax.axis_index("hid") * share
    limits = lax.dynamic_slice_in_dim(counts, first, share, 0) * BLOCK
    mixed = jnp.where(columns[None, :] < limits[:, None], summed[1], summed[0])
    full = lax.all_gather(mixed, "hid", axis=0, tiled=True)
    return lax.psum_scatter(
        lax.dot_general(
            full,
            rotation,
            (((1,), (1,)), ((), ())),
            precision=highest,
            preferred_element_type=jnp.float32,
        ),
        "tok",
        scatter_dimension=0,
        tiled=True,
    )


def solution(mesh):
    return jax.shard_map(
        local,
        mesh=mesh,
        in_specs=(P("tok", "hid"), P("tok", "hid"), P(), P(), P("hid", "tok")),
        out_specs=P("tok", "hid"),
        check_vma=False,
    )
```

profile of v0, /device:TPU:1, one launch (start us, length us, event | category | flops | bytes accessed | tf_op | source)
XLA Modules:
  0.0 485.1 jit_solution(1636365426986874242)
XLA Ops:
  6.5 1.9 pad_maximum_fusion
  8.4 0.0 all-gather.3.cloned.1.call-update
  8.4 0.0 reduce-scatter.4.cloned.1.call-start
  8.5 0.7 compare_and_fusion
  9.2 0.7 fusion.2
  9.9 109.6 %all-gather.3.cloned.1.call-done = f32[2,1024,2048]{2,1,0:T(8,128)} async-done(((f32[2,32,2048]{2,1,0:T(8,128)}), f32[2,1024,2048]{2,1,0:T(8,128)}) %all-gather.3.cloned.1.call-update) | async-done | bytes 16777232 | tf_op jit(solution)/shard_map/all_gather | solution.py:14
  119.4 32.0 %fusion = f32[2,1024,512]{2,1,0:T(8,128)S(1)} fusion(f32[2,1024,2048]{2,1,0:T(8,128)} %all-gather.3.cloned.1.call-done, f32[2048,512]{1,0:T(8,128)} %param.9), kind=kOutput, calls=%fused_computation.1 | convolution fusion | flops 25769803776 | bytes 25165824 | tf_op jit(solution)/shard_map/srk,kc->src/dot_general | solution.py:12
  151.4 1.8 slice_bitcast_fusion
  153.2 4.8 gather_fusion
  158.1 3.1 broadcast_select_fusion
  161.2 0.0 reduce-scatter.4.cloned.1.call-update
  161.2 0.0 reduce-scatter.6.cloned.1.call-start
  161.3 0.7 reduce-scatter.6.cloned.1.call-update
  161.9 0.0 all-gather.5.cloned.1.call-start
  162.0 0.8 dynamic-slice_multiply_fusion
  162.8 64.6 %reduce-scatter.4.cloned.1.call-done = f32[128,512]{1,0:T(8,128)} async-done(((f32[1024,512]{1,0:T(8,128)}), f32[128,512]{1,0:T(8,128)}) %reduce-scatter.4.cloned.1.call-update) | async-done | bytes 262160 | tf_op jit(solution)/shard_map/reduce_scatter | solution.py:25
  227.4 56.9 %reduce-scatter.6.cloned.1.call-done = f32[128,512]{1,0:T(8,128)} async-done(((f32[1024,512]{1,0:T(8,128)}), f32[128,512]{1,0:T(8,128)}) %reduce-scatter.6.cloned.1.call-update) | async-done | bytes 262160 | tf_op jit(solution)/shard_map/reduce_scatter | solution.py:24
  284.3 1.8 compare_select_fusion
  286.1 0.0 all-gather.5.cloned.1.call-update
  286.1 0.2 reduce-scatter.8.cloned.1.call-start
  286.4 53.8 %all-gather.5.cloned.1.call-done = f32[1024,512]{1,0:T(8,128)} async-done(((f32[128,512]{1,0:T(8,128)}), f32[1024,512]{1,0:T(8,128)}) %all-gather.5.cloned.1.call-update) | async-done | bytes 2097168 | tf_op jit(solution)/shard_map/all_gather | solution.py:31
  340.2 18.0 %fusion.3 = f32[1024,2048]{1,0:T(8,128)} fusion(f32[1024,512]{1,0:T(8,128)} %all-gather.5.cloned.1.call-done, f32[2048,512]{1,0:T(8,128)} %param.9), kind=kOutput, calls=%fused_computation.13 | convolution fusion | flops 12884901888 | bytes 14680064 | tf_op jit(solution)/shard_map/dot_general | solution.py:33
  358.2 0.0 reduce-scatter.8.cloned.1.call-update
  358.2 120.3 %reduce-scatter.8.cloned.1.call-done = f32[32,2048]{1,0:T(8,128)} async-done(((f32[1024,2048]{1,0:T(8,128)}), f32[32,2048]{1,0:T(8,128)}) %reduce-scatter.8.cloned.1.call-update) | async-done | bytes 262160 | tf_op jit(solution)/shard_map/reduce_scatter | solution.py:32
  (2 shorter events, 0.0 us)
Async XLA Ops:
  6.5 112.9 %all-gather.3.cloned.1.call-start = ((), (), s32[]{:S(2)}) async-start(), calls=%async_computation.3 | async-start | bytes 17301504 | tf_op jit(solution)/shard_map/all_gather | solution.py:14
  8.4 219.0 %reduce-scatter.4.cloned.1.call-start = ((), (), s32[]{:S(2)}) async-start(), calls=%async_computation.4 | async-start | bytes 2359296 | tf_op jit(solution)/shard_map/reduce_scatter | solution.py:25
  161.2 123.1 %reduce-scatter.6.cloned.1.call-start = ((), (), s32[]{:S(2)}) async-start(), calls=%async_computation.5 | async-start | bytes 2359296 | tf_op jit(solution)/shard_map/reduce_scatter | solution.py:24
  161.9 178.3 %all-gather.5.cloned.1.call-start = ((), (), s32[]{:S(2)}) async-start(), calls=%async_computation.6 | async-start | bytes 2359296 | tf_op jit(solution)/shard_map/all_gather | solution.py:31
  286.1 192.4 %reduce-scatter.8.cloned.1.call-start = ((), (), s32[]{:S(2)}) async-start(), calls=%async_computation.7 | async-start | bytes 8650752 | tf_op jit(solution)/shard_map/reduce_scatter | solution.py:32
Sparse Core Ops, SparseCore 0:
  10.0 109.3 all-gather.2
  161.3 66.0 reduce-scatter.3
  230.0 54.2 reduce-scatter.5
  286.3 53.9 all-gather.4
  358.3 120.1 reduce-scatter.7
where the time goes:
time: 485 us
  waiting for transfers between devices  406 us (84%)
  matrix products  50 us (10%)
  between operations  13.2 us (3%)
  other arithmetic  8.96 us (2%)
  local copies, waits for them, and re-layouts  6.63 us (1%)
    reduce_scatter x1, waiting for transfers between devices, local(): lax.psum_scatter(lax.dot_general(full, rotation, (((1,), (1,)), ((), ()))...  120 us
    all_gather x1, waiting for transfers between devices, local(): lax.all_gather(stacked, 'tok', axis=1, tiled=True)  110 us
    reduce_scatter x1, waiting for transfers between devices, local(): lax.psum_scatter(source_terms, 'hid', scatter_dimension=0, tiled=True)  64.6 us
    reduce_scatter x1, waiting for transfers between devices, local(): lax.psum_scatter(base_terms, 'hid', scatter_dimension=0, tiled=True)  56.9 us
    all_gather x1, waiting for transfers between devices, local(): full = lax.all_gather(mixed, 'hid', axis=0, tiled=True)  53.8 us
    dot_general x1, matrix products, local(): jnp.einsum('srk,kc->src', lax.all_gather(stacked, 'tok', axis=1, tiled=Tr...  32 us
    dot_general x1, matrix products, local(): lax.dot_general(full, rotation, (((1,), (1,)), ((), ())), precision=highe...  18 us
  transfers between devices with their start and end apart: 5, of which 5 were waited for; matrix products, arithmetic and copies ran while one was open for 0% of the time, Pallas kernels for 0%

commit v1 on v0

v1 whole, which is shorter than its diff:
```python
import jax
import jax.numpy as jnp
from jax import lax
from jax.sharding import PartitionSpec as P

BLOCK = 128


def local(base, source, pairs, counts, rotation):
    high = lax.Precision.HIGH
    stacked = jnp.stack([base, source])
    terms = jnp.einsum(
        "srk,kc->src",
        lax.all_gather(stacked, "tok", axis=1, tiled=True),
        rotation,
        precision=high,
        preferred_element_type=jnp.float32,
    )
    width = rotation.shape[1]
    columns = lax.axis_index("tok") * width + jnp.arange(width, dtype=jnp.int32)
    source_terms = terms[1].at[pairs].get(mode="promise_in_bounds")
    chosen = columns[None, :] < (counts * BLOCK)[:, None]
    mixed_terms = jnp.where(chosen, source_terms, terms[0])
    mixed = lax.psum_scatter(mixed_terms, "hid", scatter_dimension=0, tiled=True)
    full = lax.all_gather(mixed, "hid", axis=0, tiled=True)
    return lax.psum_scatter(
        lax.dot_general(
            full,
            rotation,
            (((1,), (1,)), ((), ())),
            precision=high,
            preferred_element_type=jnp.float32,
        ),
        "tok",
        scatter_dimension=0,
        tiled=True,
    )


def solution(mesh):
    return jax.shard_map(
        local,
        mesh=mesh,
        in_specs=(P("tok", "hid"), P("tok", "hid"), P(), P(), P("hid", "tok")),
        out_specs=P("tok", "hid"),
        check_vma=False,
    )
```

time: 485 us -> 408 us (0.84)
  waiting for transfers between devices: 406 us -> 351 us
  matrix products: 50 us -> 29.3 us
    reduce_scatter x2 -> x1, waiting for transfers between devices: 122 us -> 66.1 us  [local(): lax.psum_scatter(mixed_terms, 'hid', scatter_dimension=0, tiled=True)]
    dot_general x1, matrix products: 32 us -> 17.7 us  [local(): jnp.einsum('srk,kc->src', lax.all_gather(stacked, 'tok', axis=1, tiled=Tr...]
    dot_general x1, matrix products: 18 us -> 11.6 us  [local(): lax.dot_general(full, rotation, (((1,), (1,)), ((), ())), precision=high,...]
  transfers between devices with their start and end apart: 5 -> 4, of which waited for: 5 -> 4; matrix products, arithmetic and copies ran while one was open for 0% -> 0% of each run, Pallas kernels for 0% -> 0%
where the time goes in v1:
time: 408 us
  waiting for transfers between devices  351 us (86%)
  matrix products  29.3 us (7%)
  between operations  13.2 us (3%)
  other arithmetic  7.07 us (2%)
  local copies, waits for them, and re-layouts  6.99 us (2%)
    reduce_scatter x1, waiting for transfers between devices, local(): lax.psum_scatter(lax.dot_general(full, rotation, (((1,), (1,)), ((), ()))...  120 us
    all_gather x1, waiting for transfers between devices, local(): lax.all_gather(stacked, 'tok', axis=1, tiled=True)  110 us
    reduce_scatter x1, waiting for transfers between devices, local(): lax.psum_scatter(mixed_terms, 'hid', scatter_dimension=0, tiled=True)  66.1 us
    all_gather x1, waiting for transfers between devices, local(): full = lax.all_gather(mixed, 'hid', axis=0, tiled=True)  55.7 us
    dot_general x1, matrix products, local(): jnp.einsum('srk,kc->src', lax.all_gather(stacked, 'tok', axis=1, tiled=Tr...  17.7 us
    dot_general x1, matrix products, local(): lax.dot_general(full, rotation, (((1,), (1,)), ((), ())), precision=high,...  11.6 us
  transfers between devices with their start and end apart: 4, of which 4 were waited for; matrix products, arithmetic and copies ran while one was open for 0% of the time, Pallas kernels for 0%

profile of v1, /device:TPU:1, one launch (start us, length us, event | category | flops | bytes accessed | tf_op | source)
XLA Modules:
  0.0 407.9 jit_solution(10184686571337439872)
XLA Ops:
  6.5 0.0 all-gather.3.cloned.1.call-start
  6.5 1.9 pad_maximum_fusion
  8.4 0.0 all-gather.3.cloned.1.call-update
  8.4 0.0 reduce-scatter.3.cloned.1.call-start
  8.5 0.7 fusion.3
  9.2 0.7 broadcast_multiply_fusion
  9.9 109.6 %all-gather.3.cloned.1.call-done = f32[2,1024,2048]{2,1,0:T(8,128)} async-done(((f32[2,32,2048]{2,1,0:T(8,128)}), f32[2,1024,2048]{2,1,0:T(8,128)}) %all-gather.3.cloned.1.call-update) | async-done | bytes 16777232 | tf_op jit(solution)/shard_map/all_gather | solution.py:14
  119.4 17.7 %fusion = f32[2,1024,512]{2,1,0:T(8,128)S(1)} fusion(f32[2,1024,2048]{2,1,0:T(8,128)} %all-gather.3.cloned.1.call-done, f32[2048,512]{1,0:T(8,128)} %param.9), kind=kOutput, calls=%fused_computation.1 | convolution fusion | flops 12884901888 | bytes 25165824 | tf_op jit(solution)/shard_map/srk,kc->src/dot_general | solution.py:12
  137.1 0.0 copy-start
  137.1 1.9 copy-done
  139.1 0.2 slice_bitcast_fusion.1
  139.2 4.9 %gather_fusion = f32[1024,512]{1,0:T(8,128)} fusion(f32[1024,512]{1,0:T(8,128)S(1)} %slice_bitcast_fusion.1, s32[1024]{0:T(1024)S(1)} %fusion.3), kind=kCustom, calls=%fused_computation | custom fusion | bytes 4198400 | tf_op jit(solution)/shard_map/gather | solution.py:21
  144.1 3.8 fusion.2
  147.9 0.0 reduce-scatter.3.cloned.1.call-update
  148.0 0.0 all-gather.5.cloned.1.call-start
  148.0 66.1 %reduce-scatter.3.cloned.1.call-done = f32[128,512]{1,0:T(8,128)} async-done(((f32[1024,512]{1,0:T(8,128)}), f32[128,512]{1,0:T(8,128)}) %reduce-scatter.3.cloned.1.call-update) | async-done | bytes 262160 | tf_op jit(solution)/shard_map/reduce_scatter | solution.py:24
  214.2 0.0 all-gather.5.cloned.1.call-update
  214.2 0.0 reduce-scatter.5.cloned.1.call-start
  214.2 55.7 %all-gather.5.cloned.1.call-done = f32[1024,512]{1,0:T(8,128)} async-done(((f32[128,512]{1,0:T(8,128)}), f32[1024,512]{1,0:T(8,128)}) %all-gather.5.cloned.1.call-update) | async-done | bytes 2097168 | tf_op jit(solution)/shard_map/all_gather | solution.py:25
  269.9 11.6 %fusion.4 = f32[1024,2048]{1,0:T(8,128)} fusion(f32[1024,512]{1,0:T(8,128)} %all-gather.5.cloned.1.call-done, f32[2048,512]{1,0:T(8,128)} %param.9), kind=kOutput, calls=%fused_computation.11 | convolution fusion | flops 6442450944 | bytes 14680064 | tf_op jit(solution)/shard_map/dot_general | solution.py:27
  281.5 0.0 reduce-scatter.5.cloned.1.call-update
  281.5 119.9 %reduce-scatter.5.cloned.1.call-done = f32[32,2048]{1,0:T(8,128)} async-done(((f32[1024,2048]{1,0:T(8,128)}), f32[32,2048]{1,0:T(8,128)}) %reduce-scatter.5.cloned.1.call-update) | async-done | bytes 262160 | tf_op jit(solution)/shard_map/reduce_scatter | solution.py:26
  (1 shorter events, 0.0 us)
Async XLA Ops:
  6.5 112.9 %all-gather.3.cloned.1.call-start = ((), (), s32[]{:S(2)}) async-start(), calls=%async_computation.2 | async-start | bytes 17301504 | tf_op jit(solution)/shard_map/all_gather | solution.py:14
  8.4 205.7 %reduce-scatter.3.cloned.1.call-start = ((), (), s32[]{:S(2)}) async-start(), calls=%async_computation.3 | async-start | bytes 2359296 | tf_op jit(solution)/shard_map/reduce_scatter | solution.py:24
  137.1 1.9 copy-start
  148.0 121.9 %all-gather.5.cloned.1.call-start = ((), (), s32[]{:S(2)}) async-start(), calls=%async_computation.4 | async-start | bytes 2359296 | tf_op jit(solution)/shard_map/all_gather | solution.py:25
  214.2 187.2 %reduce-scatter.5.cloned.1.call-start = ((), (), s32[]{:S(2)}) async-start(), calls=%async_computation.5 | async-start | bytes 8650752 | tf_op jit(solution)/shard_map/reduce_scatter | solution.py:26
Sparse Core Ops, SparseCore 0:
  10.0 109.3 all-gather.2
  148.1 66.0 reduce-scatter.2
  216.0 53.9 all-gather.4
  281.6 119.7 reduce-scatter.4
